TPU v7x, 128 devices: a whole 4x4x4 slice. The times are simulated.
128 devices in a mesh: group: 8 (over y, core), blk: 16 (over x, z).
Axes of the slice: x: 4, y: 4, z: 4, core: 2. Of those that a mesh axis runs over, the one named last changes fastest.
Arguments:
- gradient: bfloat16 [128, 512, 2304], P(None, ('group', 'blk')), may hold values from -60 to 60
- momentum: float32 [128, 512, 2304], P(None, ('group', 'blk')), may hold values from -3 to 3
- owner_group: int32 [128, 1], replicated, may hold values from 0 to 7; in each aligned block of 128 rows (0 to 127, 128 to 255, ...) at most 32 rows name the same one
Outputs:
- update: bfloat16 [128, 512, 2304], P(None, ('group', 'blk'))
- momentum_out: float32 [128, 512, 2304], P(None, ('group', 'blk'))
- slot_rms: float32 [8, 32], P('group', 'blk')
Inputs may be any that keep to these rules, and one draw needn't show every extreme that they name: `owner_group`: each group is named by at most 32 matrices, and one group by exactly that many.
All inputs are finite; a program needn't handle non-finite values.
Results may differ from a plain program's by a relative error of at most 0.02.
Values may be sent and summed in bfloat16 or wider, within the bound.
A program may use at most 128 MiB of HBM per device.

v0:
```python
import functools
import math

import jax
import jax.numpy as jnp
from jax import lax
from jax.experimental import pallas as pl
from jax.experimental.pallas import tpu as pltpu
from jax.sharding import PartitionSpec as P

ITERS = 5
SLOTS = 2
linear_coefficient = 3.4445
coef_b = -4.775
coef_c = 2.0315
decay_rate = 0.95
epsilon = 1e-06

MESH = pl.DeviceIdType.MESH
F32 = jnp.float32
BF16 = jnp.bfloat16
LANES = 128
CHUNKS = 8


def hops(offset):
    return sum(min(step, 4 - step) for step in offset[:3])


def offsets_far_first():
    every = []
    for i in range(64):
        a, b, c = i % 4, (i // 4) % 4, i // 16
        for dcore in range(2):
            every.append((a, (a + b) % 4, (3 * a + c) % 4, (dcore + a) % 2))
    every.remove((0, 0, 0, 0))
    return sorted(every, key=hops, reverse=True)


SEND_ORDER = offsets_far_first()


def shifted(offset):
    group, blk = lax.axis_index("group"), lax.axis_index("blk")
    dx, dy, dz, dcore = offset
    y = lax.rem(group // 2 + dy, 4)
    core = lax.rem(lax.rem(group, 2) + dcore, 2)
    x = lax.rem(blk // 4 + dx, 4)
    z = lax.rem(lax.rem(blk, 4) + dz, 4)
    return (y * 2 + core, x * 4 + z)


def slot_of(offset):
    dx, dy, dz, dcore = offset
    return ((dx * 4 + dy) * 4 + dz) * 2 + dcore


def eye(size):
    rows = lax.broadcasted_iota(jnp.int32, (size, size), 0)
    return rows == lax.broadcasted_iota(jnp.int32, (size, size), 1)


def diagonals(matrix):
    size = matrix.shape[0]
    on = eye(LANES)
    columns, rows = [], []
    for i in range(0, size, LANES):
        block = jnp.where(on, matrix[i : i + LANES, i : i + LANES], 0.0)
        columns.append(jnp.sum(block, axis=1, keepdims=True))
        rows.append(jnp.sum(block, axis=0, keepdims=True))
    return jnp.concatenate(columns, 0), jnp.concatenate(rows, 1)


def parted(matrix):
    column, row = diagonals(matrix)
    off = jnp.where(eye(matrix.shape[0]), 0.0, matrix)
    return matrix, off, off.astype(BF16), column, row


def times(left, right):
    inner = jnp.dot(left[2], right[2], preferred_element_type=F32)
    return inner + left[3] * right[0] + left[1] * right[4]


def polynomial_chain(gram_ref, factor_ref, turn_ref):
    for step in range(ITERS):
        gram = parted(gram_ref[...])
        square = times(gram, gram)
        one = jnp.where(eye(square.shape[0]), linear_coefficient, 0.0)
        poly = parted(coef_b * gram[0] + coef_c * square + one)
        last = step == ITERS - 1
        if not last:
            turn_ref[...] = times(poly, gram)
        if step == 0:
            factor_ref[...] = poly[0]
        else:
            factor_ref[...] = times(poly, parted(factor_ref[...]))
        if not last:
            gram_ref[...] = times(poly, parted(turn_ref[...]))


def kernel(
    gradient,
    momentum,
    owners_ref,
    update,
    momentum_out,
    slot_ref,
    grad_v,
    mom_v,
    tx,
    rx,
    tx2,
    rx2,
    upd_v,
    norms,
    gram_ref,
    factor_ref,
    turn_ref,
    grad_sem,
    mom_sem,
    out_sem,
    upd_sem,
    send_sem,
    recv_sem,
    send2_sem,
    recv2_sem,
    own_sem,
    norm_send,
    norm_recv,
    near_sem,
):
    group, blk = lax.axis_index("group"), lax.axis_index("blk")
    me = group * 16 + blk
    count, rows, width = grad_v.shape
    tiles = width // LANES
    full_rows = rows * count
    per = count // CHUNKS

    def load(c):
        part = pl.ds(c * per, per)
        return (
            pltpu.make_async_copy(gradient.at[part], grad_v.at[part], grad_sem.at[c]),
            pltpu.make_async_copy(momentum.at[part], mom_v.at[part], mom_sem.at[c]),
        )

    def store(c):
        part = pl.ds(c * per, per)
        return pltpu.make_async_copy(mom_v.at[part], momentum_out.at[part], out_sem.at[c])

    for c in range(CHUNKS):
        for copy in load(c):
            copy.start()

    barrier = pltpu.get_barrier_semaphore()
    first = [(dx, 0, 0, dc) for dx in range(4) for dc in range(2) if (dx, dc) != (0, 0)]
    second = [(0, dy, dz, 0) for dy in range(4) for dz in range(4) if (dy, dz) != (0, 0)]
    for offset in first + second:
        pl.semaphore_signal(barrier, inc=1, device_id=shifted(offset), device_id_type=MESH)

    def ready(c):
        for copy in load(c):
            copy.wait()

        @pl.loop(0, per)
        def _(i):
            m = c * per + i
            for j in range(tiles):
                lanes = pl.ds(j * LANES, LANES)
                new = decay_rate * mom_v[m, :, lanes] + grad_v[m, :, lanes].astype(F32)
                mom_v[m, :, lanes] = new
                tx[m, j] = new.astype(BF16)

        store(c).start()

    for c in range(CHUNKS // 2):
        ready(c)
    pl.semaphore_wait(barrier, len(first) + len(second))
    for offset in second:
        pl.semaphore_signal(near_sem, inc=1, device_id=shifted(offset), device_id_type=MESH)
    for c in range(CHUNKS // 2, CHUNKS):
        ready(c)
    pl.semaphore_wait(near_sem, len(second))

    def send(offset):
        device = shifted(offset)
        at = slot_of(offset)
        return pltpu.make_async_remote_copy(
            src_ref=tx.at[device[0] * 16 + device[1]],
            dst_ref=rx.at[:, me],
            send_sem=send_sem.at[at],
            recv_sem=recv_sem.at[at],
            device_id=device,
            device_id_type=MESH,
        )

    own = pltpu.make_async_copy(tx.at[me], rx.at[:, me], own_sem.at[0])
    own.start()
    for offset in SEND_ORDER:
        send(offset).start()

    def digits(k):
        return (k // 32, (k // 8) % 4, (k // 2) % 4, k % 2)

    own.wait()

    @pl.loop(1, count)
    def _(k):
        send(digits(k)).wait()

    x_in = rx.reshape(tiles, full_rows, LANES)
    gram = None
    for j in range(0, tiles, 2):
        pair = jnp.concatenate([x_in[j], x_in[j + 1]], axis=1)
        term = lax.dot_general(pair, pair, (((1,), (1,)), ((), ())), preferred_element_type=F32)
        gram = term if gram is None else gram + term
    norm = jnp.sqrt(jnp.sum(diagonals(gram)[1]))
    norms[me] = jnp.full((1, LANES), norm, F32)

    def spread_blk(k):
        return pltpu.make_async_remote_copy(
            src_ref=norms.at[me],
            dst_ref=norms.at[me],
            send_sem=norm_send.at[k],
            recv_sem=norm_recv.at[k],
            device_id=(group, lax.rem(blk + k, 16)),
            device_id_type=MESH,
        )

    def spread_group(k):
        part = pl.ds(group * 16, 16)
        return pltpu.make_async_remote_copy(
            src_ref=norms.at[part],
            dst_ref=norms.at[part],
            send_sem=norm_send.at[16 + k],
            recv_sem=norm_recv.at[16 + k],
            device_id=(lax.rem(group + k, 8), blk),
            device_id_type=MESH,
        )

    @pl.loop(1, 16)
    def _(k):
        spread_blk(k).start()

    inverse = 1.0 / (jnp.full((1, 1), norm, F32) + epsilon)
    gram_ref[...] = gram * (inverse * inverse)
    polynomial_chain(gram_ref, factor_ref, turn_ref)

    @pl.loop(1, 16)
    def _(k):
        spread_blk(k).wait()

    @pl.loop(1, 8)
    def _(k):
        spread_group(k).start()

    factor = parted(factor_ref[...])
    scale = 0.2 * math.sqrt(max(full_rows, width))
    x_out = tx2.reshape(tiles, full_rows, LANES)
    for j in range(0, tiles, 2):
        pair = jnp.concatenate([x_in[j], x_in[j + 1]], axis=1)
        mixed = jnp.dot(factor[2], pair, preferred_element_type=F32)
        final = ((mixed + factor[3] * pair.astype(F32)) * inverse).astype(BF16)
        scaled = (scale * final.astype(F32)).astype(BF16)
        x_out[j] = scaled[:, :LANES]
        x_out[j + 1] = scaled[:, LANES:]

    def back(offset):
        device = shifted(offset)
        at = slot_of(offset)
        return pltpu.make_async_remote_copy(
            src_ref=tx2.at[:, device[0] * 16 + device[1]],
            dst_ref=rx2.at[me],
            send_sem=send2_sem.at[at],
            recv_sem=recv2_sem.at[at],
            device_id=device,
            device_id_type=MESH,
        )

    own2 = pltpu.make_async_copy(tx2.at[:, me], rx2.at[me], own_sem.at[1])
    own2.start()
    for offset in SEND_ORDER:
        back(offset).start()

    @pl.loop(1, 8)
    def _(k):
        spread_group(k).wait()

    owner = jnp.broadcast_to(owners_ref[...], (count, LANES))
    other = jnp.transpose(owner.astype(F32)).astype(jnp.int32)
    row = lax.broadcasted_iota(jnp.int32, (count, LANES), 0)
    lane = lax.broadcasted_iota(jnp.int32, (count, LANES), 1)
    earlier = jnp.where((owner == other) & (lane < row), 1.0, 0.0)
    rank = jnp.sum(earlier, axis=1, keepdims=True).astype(jnp.int32)
    placing = owner * (SLOTS * 16) + rank
    spread = norms[:, 0, :] * (1.0 / math.sqrt(full_rows * width))
    chosen = jnp.where(placing == me * SLOTS + lane, spread, 0.0)
    slot_ref[...] = jnp.sum(chosen, axis=0, keepdims=True)[:, :SLOTS]

    def arrived(m):
        for j in range(tiles):
            upd_v[m, :, pl.ds(j * LANES, LANES)] = rx2[m, j]

    own2.wait()
    arrived(me)

    @pl.loop(0, count - 1)
    def _(i):
        dx, dy, dz, dc = digits(count - 1 - i)
        back((dx, dy, dz, dc)).wait()
        gone = shifted(((4 - dx) % 4, (4 - dy) % 4, (4 - dz) % 4, dc))
        arrived(gone[0] * 16 + gone[1])

    done = pltpu.make_async_copy(upd_v, update, upd_sem.at[0])
    done.start()
    for c in range(CHUNKS):
        store(c).wait()
    done.wait()


def on_device(gradient, momentum, owner_group):
    count, rows, width = gradient.shape
    tiles = width // LANES
    full_rows = rows * count
    wide = (count, tiles, rows, LANES)
    tall = (tiles, count, rows, LANES)
    square = pltpu.VMEM((full_rows, full_rows), F32)
    dma = pltpu.SemaphoreType.DMA
    return pl.pallas_call(
        kernel,
        out_shape=(
            jax.ShapeDtypeStruct(gradient.shape, BF16),
            jax.ShapeDtypeStruct(momentum.shape, F32),
            jax.ShapeDtypeStruct((1, SLOTS), F32),
        ),
        in_specs=[
            pl.BlockSpec(memory_space=pl.ANY),
            pl.BlockSpec(memory_space=pl.ANY),
            pl.BlockSpec(memory_space=pltpu.VMEM),
        ],
        out_specs=(
            pl.BlockSpec(memory_space=pl.ANY),
            pl.BlockSpec(memory_space=pl.ANY),
            pl.BlockSpec(memory_space=pltpu.VMEM),
        ),
        scratch_shapes=[
            pltpu.VMEM(gradient.shape, BF16),
            pltpu.VMEM(momentum.shape, F32),
            pltpu.VMEM(wide, BF16),
            pltpu.VMEM(tall, BF16),
            pltpu.VMEM(tall, BF16),
            pltpu.VMEM(wide, BF16),
            pltpu.VMEM(gradient.shape, BF16),
            pltpu.VMEM((count, 1, LANES), F32),
            square,
            square,
            square,
            dma((CHUNKS,)),
            dma((CHUNKS,)),
            dma((CHUNKS,)),
            dma((1,)),
            dma((count,)),
            dma((count,)),
            dma((count,)),
            dma((count,)),
            dma((2,)),
            dma((24,)),
            dma((24,)),
            pltpu.SemaphoreType.REGULAR,
        ],
        compiler_params=pltpu.CompilerParams(
            collective_id=0, has_side_effects=True, vmem_limit_bytes=50 << 20
        ),
    )(gradient, momentum, owner_group)


def solution(mesh):
    placed = (P(None, ("group", "blk"), None), P(None, ("group", "blk"), None), P())
    return jax.shard_map(
        on_device,
        mesh=mesh,
        in_specs=placed,
        out_specs=(
            P(None, ("group", "blk"), None),
            P(None, ("group", "blk"), None),
            P("group", "blk"),
        ),
        check_vma=False,
    )
```

profile of v0, /device:TPU:1, one launch (start us, length us, event | category | flops | bytes accessed | tf_op | source)
XLA Modules:
  0.0 99.7 jit_solution(7273267965447051569)
XLA Ops:
  0.6 0.8 copy.6.owners_ref
  1.4 92.4 %shard_map.58 = (bf16[128,4,2304]{2,1,0:T(4,128)(2,1)S(1)}, f32[128,4,2304]{2,1,0:T(4,128)}, f32[1,2]{1,0:T(1,128)S(1)}) custom-call(bf16[128,4,2304]{2,1,0:T(4,128)(2,1)} %gradient.1, f32[128,4,2304]{2,1,0:T(4,128)} %momentum.1, s32[128,1]{1,0:T(8,128)S(1)} %copy.6.owners_ref), custom_call_target="tpu_custom_call" | custom-call | tf_op jit(solution)/shard_map/pallas_call | solution.py:329
  93.8 0.0 copy-start
  93.8 1.4 %copy.10 = bf16[128,4,2304]{2,1,0:T(4,128)(2,1)} copy(bf16[128,4,2304]{2,1,0:T(4,128)(2,1)S(1)} %get-tuple-element.6) | data formatting | bytes 4718592
  95.2 1.8 %copy-done = f32[128,4,2304]{2,1,0:T(4,128)S(1)} copy-done((f32[128,4,2304]{2,1,0:T(4,128)S(1)}, f32[128,4,2304]{2,1,0:T(4,128)}, u32[]{:S(2)}) %copy-start) | copy-done | bytes 4718616
  97.0 2.2 %copy.11 = f32[128,4,2304]{2,1,0:T(4,128)} copy(f32[128,4,2304]{2,1,0:T(4,128)S(1)} %copy-done) | data formatting | bytes 9437184
  99.2 0.5 copy.12
Async XLA Ops:
  93.8 3.2 %copy-start = (f32[128,4,2304]{2,1,0:T(4,128)S(1)}, f32[128,4,2304]{2,1,0:T(4,128)}, u32[]{:S(2)}) copy-start(f32[128,4,2304]{2,1,0:T(4,128)} %get-tuple-element.7) | copy-start | bytes 14155780
where the time goes:
time: 99.9 us; the launch traced here: 99.7 us
  Pallas kernels  92.4 us (92%)
  local copies, waits for them, and re-layouts  6.64 us (7%)
    pallas_call x1, Pallas kernels, on_device(): pl.pallas_call(kernel, out_shape=(jax.ShapeDtypeStruct(gradient.shape, BF...  92.4 us
    unnamed x6, local copies, waits for them, and re-layouts  6.64 us

commit v1 on v0

--- a/solution.py
+++ b/solution.py
@@ -20,24 +20,22 @@
 F32 = jnp.float32
 BF16 = jnp.bfloat16
 LANES = 128
-CHUNKS = 8
+CHUNKS = 4
 
 
 def hops(offset):
-    return sum(min(step, 4 - step) for step in offset[:3])
-
-
-def offsets_far_first():
+    return sum(min(step, 4 - step) for step in offset)
+
+
+def chips_far_first():
     every = []
-    for i in range(64):
+    for i in range(1, 64):
         a, b, c = i % 4, (i // 4) % 4, i // 16
-        for dcore in range(2):
-            every.append((a, (a + b) % 4, (3 * a + c) % 4, (dcore + a) % 2))
-    every.remove((0, 0, 0, 0))
+        every.append((a, (a + b) % 4, (3 * a + c) % 4))
     return sorted(every, key=hops, reverse=True)
 
 
-SEND_ORDER = offsets_far_first()
+CHIP_ORDER = chips_far_first()
 
 
 def shifted(offset):
@@ -50,9 +48,9 @@
     return (y * 2 + core, x * 4 + z)
 
 
-def slot_of(offset):
-    dx, dy, dz, dcore = offset
-    return ((dx * 4 + dy) * 4 + dz) * 2 + dcore
+def row_of(offset):
+    dx, dy, _, dcore = offset
+    return (dx * 4 + dy) * 2 + dcore
 
 
 def eye(size):
@@ -103,24 +101,20 @@
     gradient,
     momentum,
     owners_ref,
-    update,
-    momentum_out,
+    upd_v,
+    mom_v,
     slot_ref,
     grad_v,
-    mom_v,
     tx,
     rx,
     tx2,
     rx2,
-    upd_v,
     norms,
     gram_ref,
     factor_ref,
     turn_ref,
     grad_sem,
     mom_sem,
-    out_sem,
-    upd_sem,
     send_sem,
     recv_sem,
     send2_sem,
@@ -128,10 +122,10 @@
     own_sem,
     norm_send,
     norm_recv,
-    near_sem,
 ):
     group, blk = lax.axis_index("group"), lax.axis_index("blk")
     me = group * 16 + blk
+    core = lax.rem(group, 2)
     count, rows, width = grad_v.shape
     tiles = width // LANES
     full_rows = rows * count
@@ -144,19 +138,17 @@
             pltpu.make_async_copy(momentum.at[part], mom_v.at[part], mom_sem.at[c]),
         )
 
-    def store(c):
-        part = pl.ds(c * per, per)
-        return pltpu.make_async_copy(mom_v.at[part], momentum_out.at[part], out_sem.at[c])
-
     for c in range(CHUNKS):
         for copy in load(c):
             copy.start()
 
     barrier = pltpu.get_barrier_semaphore()
-    first = [(dx, 0, 0, dc) for dx in range(4) for dc in range(2) if (dx, dc) != (0, 0)]
-    second = [(0, dy, dz, 0) for dy in range(4) for dz in range(4) if (dy, dz) != (0, 0)]
-    for offset in first + second:
-        pl.semaphore_signal(barrier, inc=1, device_id=shifted(offset), device_id_type=MESH)
+
+    def digits(k):
+        return (k // 32, (k // 8) % 4, (k // 2) % 4, k % 2)
+
+    for k in range(1, count):
+        pl.semaphore_signal(barrier, inc=1, device_id=shifted(digits(k)), device_id_type=MESH)
 
     def ready(c):
         for copy in load(c):
@@ -171,42 +163,43 @@
                 mom_v[m, :, lanes] = new
                 tx[m, j] = new.astype(BF16)
 
-        store(c).start()
-
-    for c in range(CHUNKS // 2):
+    for c in range(CHUNKS):
         ready(c)
-    pl.semaphore_wait(barrier, len(first) + len(second))
-    for offset in second:
-        pl.semaphore_signal(near_sem, inc=1, device_id=shifted(offset), device_id_type=MESH)
-    for c in range(CHUNKS // 2, CHUNKS):
-        ready(c)
-    pl.semaphore_wait(near_sem, len(second))
-
-    def send(offset):
+    pl.semaphore_wait(barrier, count - 1)
+
+    def send(offset, wave):
         device = shifted(offset)
-        at = slot_of(offset)
         return pltpu.make_async_remote_copy(
             src_ref=tx.at[device[0] * 16 + device[1]],
             dst_ref=rx.at[:, me],
-            send_sem=send_sem.at[at],
-            recv_sem=recv_sem.at[at],
+            send_sem=send_sem.at[wave],
+            recv_sem=recv_sem.at[0],
             device_id=device,
             device_id_type=MESH,
         )
 
     own = pltpu.make_async_copy(tx.at[me], rx.at[:, me], own_sem.at[0])
     own.start()
-    for offset in SEND_ORDER:
-        send(offset).start()
-
-    def digits(k):
-        return (k // 32, (k // 8) % 4, (k // 2) % 4, k % 2)
+    def sent(blocks, sem):
+        part = tx.at[pl.ds(0, blocks)]
+        return pltpu.make_async_remote_copy(
+            src_ref=part,
+            dst_ref=part,
+            send_sem=sem,
+            recv_sem=recv_sem.at[0],
+            device_id=(group, blk),
+            device_id_type=MESH,
+        )
+
+    for wave in range(2):
+        for chip in CHIP_ORDER:
+            send((*chip, lax.rem(core + wave, 2)), wave).start()
+        if wave == 0:
+            sent(count // 2 - 1, send_sem.at[0]).wait_send()
+    send((0, 0, 0, 1), 1).start()
 
     own.wait()
-
-    @pl.loop(1, count)
-    def _(k):
-        send(digits(k)).wait()
+    sent(count - 1, send_sem.at[1]).wait_recv()
 
     x_in = rx.reshape(tiles, full_rows, LANES)
     gram = None
@@ -221,8 +214,8 @@
         return pltpu.make_async_remote_copy(
             src_ref=norms.at[me],
             dst_ref=norms.at[me],
-            send_sem=norm_send.at[k],
-            recv_sem=norm_recv.at[k],
+            send_sem=norm_send.at[0],
+            recv_sem=norm_recv.at[0],
             device_id=(group, lax.rem(blk + k, 16)),
             device_id_type=MESH,
         )
@@ -232,27 +225,29 @@
         return pltpu.make_async_remote_copy(
             src_ref=norms.at[part],
             dst_ref=norms.at[part],
-            send_sem=norm_send.at[16 + k],
-            recv_sem=norm_recv.at[16 + k],
+            send_sem=norm_send.at[1],
+            recv_sem=norm_recv.at[1],
             device_id=(lax.rem(group + k, 8), blk),
             device_id_type=MESH,
         )
 
-    @pl.loop(1, 16)
-    def _(k):
+    def spread_all(blocks, at):
+        part = norms.at[pl.ds(0, blocks)]
+        return pltpu.make_async_remote_copy(
+            src_ref=part,
+            dst_ref=part,
+            send_sem=norm_send.at[at],
+            recv_sem=norm_recv.at[at],
+            device_id=(group, blk),
+            device_id_type=MESH,
+        )
+
+    for k in range(1, 16):
         spread_blk(k).start()
 
     inverse = 1.0 / (jnp.full((1, 1), norm, F32) + epsilon)
     gram_ref[...] = gram * (inverse * inverse)
     polynomial_chain(gram_ref, factor_ref, turn_ref)
-
-    @pl.loop(1, 16)
-    def _(k):
-        spread_blk(k).wait()
-
-    @pl.loop(1, 8)
-    def _(k):
-        spread_group(k).start()
 
     factor = parted(factor_ref[...])
     scale = 0.2 * math.sqrt(max(full_rows, width))
@@ -267,27 +262,62 @@
 
     def back(offset):
         device = shifted(offset)
-        at = slot_of(offset)
         return pltpu.make_async_remote_copy(
             src_ref=tx2.at[:, device[0] * 16 + device[1]],
             dst_ref=rx2.at[me],
-            send_sem=send2_sem.at[at],
-            recv_sem=recv2_sem.at[at],
+            send_sem=send2_sem.at[0],
+            recv_sem=recv2_sem.at[row_of(offset)],
             device_id=device,
             device_id_type=MESH,
         )
 
     own2 = pltpu.make_async_copy(tx2.at[:, me], rx2.at[me], own_sem.at[1])
     own2.start()
-    for offset in SEND_ORDER:
-        back(offset).start()
-
-    @pl.loop(1, 8)
-    def _(k):
-        spread_group(k).wait()
-
-    owner = jnp.broadcast_to(owners_ref[...], (count, LANES))
-    other = jnp.transpose(owner.astype(F32)).astype(jnp.int32)
+    for chip in CHIP_ORDER:
+        for other_core in range(2):
+            back((*chip, other_core)).start()
+    back((0, 0, 0, 1)).start()
+
+    spread_all(15, 0).wait()
+    for k in range(1, 8):
+        spread_group(k).start()
+
+    def arrived(m):
+        for j in range(tiles):
+            upd_v[m, :, pl.ds(j * LANES, LANES)] = rx2[m, j]
+
+    def row_arrived(dx, dy, dcore, steps):
+        part = rx2.at[pl.ds(0, len(steps))]
+        pltpu.make_async_remote_copy(
+            src_ref=part,
+            dst_ref=part,
+            send_sem=send2_sem.at[0],
+            recv_sem=recv2_sem.at[row_of((dx, dy, 0, dcore))],
+            device_id=(group, blk),
+            device_id_type=MESH,
+        ).wait_recv()
+        for dz in steps:
+            gone = shifted((lax.rem(4 - dx, 4), lax.rem(4 - dy, 4), (4 - dz) % 4, dcore))
+            arrived(gone[0] * 16 + gone[1])
+
+    for wave in range(2):
+        turn = lax.rem(core + wave, 2)
+
+        @pl.loop(0, 15)
+        def _(i):
+            row_arrived((15 - i) // 4, lax.rem(15 - i, 4), turn, (2, 1, 3, 0))
+
+        if wave == 0:
+            own2.wait()
+            arrived(me)
+
+    row_arrived(0, 0, 0, (2, 1, 3))
+    row_arrived(0, 0, 1, (2, 1, 3, 0))
+
+    spread_all(7 * 16, 1).wait()
+
+    other = jnp.broadcast_to(owners_ref[...], (count, LANES))
+    owner = jnp.transpose(other.astype(F32)).astype(jnp.int32)
     row = lax.broadcasted_iota(jnp.int32, (count, LANES), 0)
     lane = lax.broadcasted_iota(jnp.int32, (count, LANES), 1)
     earlier = jnp.where((owner == other) & (lane < row), 1.0, 0.0)
@@ -297,25 +327,8 @@
     chosen = jnp.where(placing == me * SLOTS + lane, spread, 0.0)
     slot_ref[...] = jnp.sum(chosen, axis=0, keepdims=True)[:, :SLOTS]
 
-    def arrived(m):
-        for j in range(tiles):
-            upd_v[m, :, pl.ds(j * LANES, LANES)] = rx2[m, j]
-
-    own2.wait()
-    arrived(me)
-
-    @pl.loop(0, count - 1)
-    def _(i):
-        dx, dy, dz, dc = digits(count - 1 - i)
-        back((dx, dy, dz, dc)).wait()
-        gone = shifted(((4 - dx) % 4, (4 - dy) % 4, (4 - dz) % 4, dc))
-        arrived(gone[0] * 16 + gone[1])
-
-    done = pltpu.make_async_copy(upd_v, update, upd_sem.at[0])
-    done.start()
-    for c in range(CHUNKS):
-        store(c).wait()
-    done.wait()
+    sent(count // 2, send_sem.at[1]).wait_send()
+    sent(count - 1, send2_sem.at[0]).wait_send()
 
 
 def on_device(gradient, momentum, owner_group):
@@ -339,39 +352,34 @@
             pl.BlockSpec(memory_space=pltpu.VMEM),
         ],
         out_specs=(
-            pl.BlockSpec(memory_space=pl.ANY),
-            pl.BlockSpec(memory_space=pl.ANY),
+            pl.BlockSpec(memory_space=pltpu.VMEM),
+            pl.BlockSpec(memory_space=pltpu.VMEM),
             pl.BlockSpec(memory_space=pltpu.VMEM),
         ),
         scratch_shapes=[
             pltpu.VMEM(gradient.shape, BF16),
-            pltpu.VMEM(momentum.shape, F32),
             pltpu.VMEM(wide, BF16),
             pltpu.VMEM(tall, BF16),
             pltpu.VMEM(tall, BF16),
             pltpu.VMEM(wide, BF16),
-            pltpu.VMEM(gradient.shape, BF16),
             pltpu.VMEM((count, 1, LANES), F32),
             square,
             square,
             square,
             dma((CHUNKS,)),
             dma((CHUNKS,)),
-            dma((CHUNKS,)),
+            dma((2,)),
             dma((1,)),
-            dma((count,)),
-            dma((count,)),
-            dma((count,)),
-            dma((count,)),
+            dma((1,)),
+            dma((32,)),
             dma((2,)),
-            dma((24,)),
-            dma((24,)),
-            pltpu.SemaphoreType.REGULAR,
+            dma((2,)),
+            dma((2,)),
         ],
         compiler_params=pltpu.CompilerParams(
-            collective_id=0, has_side_effects=True, vmem_limit_bytes=50 << 20
+            collective_id=0, has_side_effects=True, vmem_limit_bytes=44 << 20
         ),
-    )(gradient, momentum, owner_group)
+    )(gradient, momentum, owner_group.reshape(1, count))
 
 
 def solution(mesh):

time: 99.9 us -> 76.4 us (0.76)
  Pallas kernels: 92.4 us -> 69.1 us
    pallas_call x1, Pallas kernels: 92.4 us -> 69.1 us  [on_device(): pl.pallas_call(kernel, out_shape=(jax.ShapeDtypeStruct(gradient.shape, BF...]
    unnamed x6 -> x7, local copies, waits for them, and re-layouts: 6.64 us -> 6.42 us
where the time goes in v1:
time: 76.4 us; the launch traced here: 76.2 us
  Pallas kernels  69.1 us (90%)
  local copies, waits for them, and re-layouts  6.42 us (8%)
    pallas_call x1, Pallas kernels, on_device(): pl.pallas_call(kernel, out_shape=(jax.ShapeDtypeStruct(gradient.shape, BF...  69.1 us
    unnamed x7, local copies, waits for them, and re-layouts  6.42 us

profile of v1, /device:TPU:1, one launch (start us, length us, event | category | flops | bytes accessed | tf_op | source)
XLA Modules:
  0.0 76.2 jit_solution(7407428050048570875)
XLA Ops:
  0.6 0.0 copy-start
  0.6 1.7 %copy-done = bf16[128,4,2304]{2,1,0:T(4,128)(2,1)S(1)} copy-done((bf16[128,4,2304]{2,1,0:T(4,128)(2,1)S(1)}, bf16[128,4,2304]{2,1,0:T(4,128)(2,1)}, u32[]{:S(2)}) %copy-start) | copy-done | bytes 2359320
  2.3 0.0 copy-start.1
  2.3 0.7 copy-done.1
  3.0 69.1 %shard_map.58 = (bf16[128,4,2304]{2,1,0:T(4,128)(2,1)S(1)}, f32[128,4,2304]{2,1,0:T(4,128)S(1)}, f32[1,2]{1,0:T(1,128)S(1)}) custom-call(bf16[128,4,2304]{2,1,0:T(4,128)(2,1)S(1)} %copy-done, f32[128,4,2304]{2,1,0:T(4,128)} %momentum.1, s32[1,128]{1,0:T(1,128)S(1)} %bitcast.1), custom_call_target="tpu_custom_call" | custom-call | tf_op jit(solution)/shard_map/pallas_call | solution.py:342
  72.1 1.4 %copy.9 = bf16[128,4,2304]{2,1,0:T(4,128)(2,1)} copy(bf16[128,4,2304]{2,1,0:T(4,128)(2,1)S(1)} %get-tuple-element.6) | data formatting | bytes 4718592
  73.5 2.2 %copy.10 = f32[128,4,2304]{2,1,0:T(4,128)} copy(f32[128,4,2304]{2,1,0:T(4,128)S(1)} %get-tuple-element.7) | data formatting | bytes 9437184
  75.7 0.5 copy.11
Async XLA Ops:
  0.6 1.7 %copy-start = (bf16[128,4,2304]{2,1,0:T(4,128)(2,1)S(1)}, bf16[128,4,2304]{2,1,0:T(4,128)(2,1)}, u32[]{:S(2)}) copy-start(bf16[128,4,2304]{2,1,0:T(4,128)(2,1)} %gradient.1) | copy-start | bytes 7077892
  2.3 0.7 copy-start.1

commit v2 on v1

--- a/solution.py
+++ b/solution.py
@@ -20,7 +20,7 @@
 F32 = jnp.float32
 BF16 = jnp.bfloat16
 LANES = 128
-CHUNKS = 4
+CHUNKS = 8
 
 
 def hops(offset):
@@ -36,6 +36,7 @@
 
 
 CHIP_ORDER = chips_far_first()
+AHEAD = 63
 
 
 def shifted(offset):
@@ -46,6 +47,16 @@
     x = lax.rem(blk // 4 + dx, 4)
     z = lax.rem(lax.rem(blk, 4) + dz, 4)
     return (y * 2 + core, x * 4 + z)
+
+
+def coordinate_tables():
+    group, blk = lax.axis_index("group"), lax.axis_index("blk")
+    doubled = [lax.rem(group // 2 + dy, 4) * 2 for dy in range(4)]
+    along_x = [lax.rem(blk // 4 + dx, 4) * 4 for dx in range(4)]
+    along_z = [lax.rem(lax.rem(blk, 4) + dz, 4) for dz in range(4)]
+    groups = [[first + c for c in range(2)] for first in doubled]
+    blks = [[first + second for second in along_z] for first in along_x]
+    return groups, blks
 
 
 def row_of(offset):
@@ -100,11 +111,12 @@
 def kernel(
     gradient,
     momentum,
-    owners_ref,
+    owners,
     upd_v,
     mom_v,
     slot_ref,
     grad_v,
+    owners_v,
     tx,
     rx,
     tx2,
@@ -122,10 +134,13 @@
     own_sem,
     norm_send,
     norm_recv,
+    mate_sem,
+    chip_sem,
 ):
     group, blk = lax.axis_index("group"), lax.axis_index("blk")
     me = group * 16 + blk
     core = lax.rem(group, 2)
+    groups, blks = coordinate_tables()
     count, rows, width = grad_v.shape
     tiles = width // LANES
     full_rows = rows * count
@@ -138,17 +153,31 @@
             pltpu.make_async_copy(momentum.at[part], mom_v.at[part], mom_sem.at[c]),
         )
 
-    for c in range(CHUNKS):
+    for c in range(0, CHUNKS, 2):
         for copy in load(c):
             copy.start()
 
+    owners_copy = pltpu.make_async_copy(owners, owners_v, own_sem.at[2])
+    owners_copy.start()
     barrier = pltpu.get_barrier_semaphore()
 
     def digits(k):
         return (k // 32, (k // 8) % 4, (k // 2) % 4, k % 2)
 
-    for k in range(1, count):
-        pl.semaphore_signal(barrier, inc=1, device_id=shifted(digits(k)), device_id_type=MESH)
+    def device_at(chip, which):
+        dx, dy, dz = chip
+        return (groups[dy][which], blks[dx][dz])
+
+    @pl.when(core == 0)
+    def _():
+        for chip in CHIP_ORDER:
+            pl.semaphore_signal(
+                barrier, inc=1, device_id=device_at(chip, 0), device_id_type=MESH
+            )
+
+    for c in range(1, CHUNKS, 2):
+        for copy in load(c):
+            copy.start()
 
     def ready(c):
         for copy in load(c):
@@ -163,23 +192,32 @@
                 mom_v[m, :, lanes] = new
                 tx[m, j] = new.astype(BF16)
 
-    for c in range(CHUNKS):
+    for c in range(0, CHUNKS, 2):
         ready(c)
-    pl.semaphore_wait(barrier, count - 1)
-
-    def send(offset, wave):
-        device = shifted(offset)
+    mate = shifted((0, 0, 0, 1))
+
+    @pl.when(core == 0)
+    def _():
+        pl.semaphore_wait(barrier, len(CHIP_ORDER))
+        pl.semaphore_signal(barrier, inc=1, device_id=mate, device_id_type=MESH)
+
+    @pl.when(core == 1)
+    def _():
+        pl.semaphore_wait(barrier, 1)
+        pl.semaphore_signal(mate_sem, inc=1, device_id=mate, device_id_type=MESH)
+
+    def send(device, send_sem):
         return pltpu.make_async_remote_copy(
             src_ref=tx.at[device[0] * 16 + device[1]],
             dst_ref=rx.at[:, me],
-            send_sem=send_sem.at[wave],
+            send_sem=send_sem,
             recv_sem=recv_sem.at[0],
             device_id=device,
             device_id_type=MESH,
         )
 
     own = pltpu.make_async_copy(tx.at[me], rx.at[:, me], own_sem.at[0])
-    own.start()
+
     def sent(blocks, sem):
         part = tx.at[pl.ds(0, blocks)]
         return pltpu.make_async_remote_copy(
@@ -191,12 +229,40 @@
             device_id_type=MESH,
         )
 
-    for wave in range(2):
-        for chip in CHIP_ORDER:
-            send((*chip, lax.rem(core + wave, 2)), wave).start()
-        if wave == 0:
-            sent(count // 2 - 1, send_sem.at[0]).wait_send()
-    send((0, 0, 0, 1), 1).start()
+    def all_in():
+        @pl.when(core == 0)
+        def _():
+            pl.semaphore_wait(mate_sem, 1)
+            for chip in CHIP_ORDER:
+                pl.semaphore_signal(
+                    chip_sem, inc=1, device_id=device_at(chip, 0), device_id_type=MESH
+                )
+            pl.semaphore_wait(chip_sem, len(CHIP_ORDER))
+            pl.semaphore_signal(mate_sem, inc=1, device_id=mate, device_id_type=MESH)
+
+        @pl.when(core == 1)
+        def _():
+            pl.semaphore_wait(mate_sem, 1)
+
+    for i, chip in enumerate(CHIP_ORDER):
+        send(device_at(chip, 0), send_sem.at[0 if i < AHEAD else 1]).start()
+
+    @pl.when(core == 1)
+    def _():
+        send(mate, send_sem.at[2]).start()
+
+    for c in range(1, CHUNKS, 2):
+        ready(c)
+    own.start()
+    all_in()
+
+    @pl.when(core == 0)
+    def _():
+        send(mate, send_sem.at[2]).start()
+
+    sent(AHEAD, send_sem.at[0]).wait_send()
+    for chip in CHIP_ORDER:
+        send(device_at(chip, 1), send_sem.at[1]).start()
 
     own.wait()
     sent(count - 1, send_sem.at[1]).wait_recv()
@@ -300,6 +366,21 @@
             gone = shifted((lax.rem(4 - dx, 4), lax.rem(4 - dy, 4), (4 - dz) % 4, dcore))
             arrived(gone[0] * 16 + gone[1])
 
+    def fill_slots():
+        spread_all(7 * 16, 1).wait()
+
+        owners_copy.wait()
+        other = jnp.broadcast_to(owners_v[...], (count, LANES))
+        owner = jnp.transpose(other.astype(F32)).astype(jnp.int32)
+        row = lax.broadcasted_iota(jnp.int32, (count, LANES), 0)
+        lane = lax.broadcasted_iota(jnp.int32, (count, LANES), 1)
+        earlier = jnp.where((owner == other) & (lane < row), 1.0, 0.0)
+        rank = jnp.sum(earlier, axis=1, keepdims=True).astype(jnp.int32)
+        placing = owner * (SLOTS * 16) + rank
+        spread = norms[:, 0, :] * (1.0 / math.sqrt(full_rows * width))
+        chosen = jnp.where(placing == me * SLOTS + lane, spread, 0.0)
+        slot_ref[...] = jnp.sum(chosen, axis=0, keepdims=True)[:, :SLOTS]
+
     for wave in range(2):
         turn = lax.rem(core + wave, 2)
 
@@ -310,25 +391,18 @@
         if wave == 0:
             own2.wait()
             arrived(me)
+            fill_slots()
 
     row_arrived(0, 0, 0, (2, 1, 3))
     row_arrived(0, 0, 1, (2, 1, 3, 0))
 
-    spread_all(7 * 16, 1).wait()
-
-    other = jnp.broadcast_to(owners_ref[...], (count, LANES))
-    owner = jnp.transpose(other.astype(F32)).astype(jnp.int32)
-    row = lax.broadcasted_iota(jnp.int32, (count, LANES), 0)
-    lane = lax.broadcasted_iota(jnp.int32, (count, LANES), 1)
-    earlier = jnp.where((owner == other) & (lane < row), 1.0, 0.0)
-    rank = jnp.sum(earlier, axis=1, keepdims=True).astype(jnp.int32)
-    placing = owner * (SLOTS * 16) + rank
-    spread = norms[:, 0, :] * (1.0 / math.sqrt(full_rows * width))
-    chosen = jnp.where(placing == me * SLOTS + lane, spread, 0.0)
-    slot_ref[...] = jnp.sum(chosen, axis=0, keepdims=True)[:, :SLOTS]
-
-    sent(count // 2, send_sem.at[1]).wait_send()
+    sent(count - 2 - AHEAD, send_sem.at[1]).wait_send()
+    sent(1, send_sem.at[2]).wait_send()
     sent(count - 1, send2_sem.at[0]).wait_send()
+
+
+def in_hbm(array):
+    return pltpu.with_memory_space_constraint(array, pltpu.HBM)
 
 
 def on_device(gradient, momentum, owner_group):
@@ -349,7 +423,7 @@
         in_specs=[
             pl.BlockSpec(memory_space=pl.ANY),
             pl.BlockSpec(memory_space=pl.ANY),
-            pl.BlockSpec(memory_space=pltpu.VMEM),
+            pl.BlockSpec(memory_space=pl.ANY),
         ],
         out_specs=(
             pl.BlockSpec(memory_space=pltpu.VMEM),
@@ -358,6 +432,7 @@
         ),
         scratch_shapes=[
             pltpu.VMEM(gradient.shape, BF16),
+            pltpu.VMEM((1, count), jnp.int32),
             pltpu.VMEM(wide, BF16),
             pltpu.VMEM(tall, BF16),
             pltpu.VMEM(tall, BF16),
@@ -368,18 +443,20 @@
             square,
             dma((CHUNKS,)),
             dma((CHUNKS,)),
-            dma((2,)),
+            dma((3,)),
             dma((1,)),
             dma((1,)),
             dma((32,)),
+            dma((3,)),
             dma((2,)),
             dma((2,)),
-            dma((2,)),
+            pltpu.SemaphoreType.REGULAR,
+            pltpu.SemaphoreType.REGULAR,
         ],
         compiler_params=pltpu.CompilerParams(
             collective_id=0, has_side_effects=True, vmem_limit_bytes=44 << 20
         ),
-    )(gradient, momentum, owner_group.reshape(1, count))
+    )(*(in_hbm(x) for x in (gradient, momentum, owner_group.reshape(1, count))))
 
 
 def solution(mesh):

time: 76.4 us -> 73.7 us (0.965)
  local copies, waits for them, and re-layouts: 6.42 us -> 4.1 us
    unnamed x7 -> x3, local copies, waits for them, and re-layouts: 6.42 us -> 4.1 us
where the time goes in v2:
time: 73.7 us; the launch traced here: 73.6 us
  Pallas kernels  68.8 us (93%)
  local copies, waits for them, and re-layouts  4.1 us (6%)
    pallas_call x1, Pallas kernels, on_device(): pl.pallas_call(kernel, out_shape=(jax.ShapeDtypeStruct(gradient.shape, BF...  68.8 us
    unnamed x3, local copies, waits for them, and re-layouts  4.1 us

profile of v2, /device:TPU:1, one launch (start us, length us, event | category | flops | bytes accessed | tf_op | source)
XLA Modules:
  0.0 73.6 jit_solution(11173306038837619985)
XLA Ops:
  0.6 68.8 %shard_map.58 = (bf16[128,4,2304]{2,1,0:T(4,128)(2,1)S(1)}, f32[128,4,2304]{2,1,0:T(4,128)S(1)}, f32[1,2]{1,0:T(1,128)S(1)}) custom-call(bf16[128,4,2304]{2,1,0:T(4,128)(2,1)} %gradient.1, f32[128,4,2304]{2,1,0:T(4,128)} %momentum.1, s32[1,128]{1,0:T(1,128)} %bitcast.1), custom_call_target="tpu_custom_call" | custom-call | tf_op jit(solution)/shard_map/pallas_call | solution.py:416
  69.5 1.4 %copy.9 = bf16[128,4,2304]{2,1,0:T(4,128)(2,1)} copy(bf16[128,4,2304]{2,1,0:T(4,128)(2,1)S(1)} %get-tuple-element.6) | data formatting | bytes 4718592
  70.9 2.2 %copy.10 = f32[128,4,2304]{2,1,0:T(4,128)} copy(f32[128,4,2304]{2,1,0:T(4,128)S(1)} %get-tuple-element.7) | data formatting | bytes 9437184
  73.1 0.5 copy.11

commit v3 on v2

--- a/solution.py
+++ b/solution.py
@@ -57,11 +57,6 @@
     groups = [[first + c for c in range(2)] for first in doubled]
     blks = [[first + second for second in along_z] for first in along_x]
     return groups, blks
-
-
-def row_of(offset):
-    dx, dy, _, dcore = offset
-    return (dx * 4 + dy) * 2 + dcore
 
 
 def eye(size):
@@ -112,7 +107,7 @@
     gradient,
     momentum,
     owners,
-    upd_v,
+    rx2,
     mom_v,
     slot_ref,
     grad_v,
@@ -120,7 +115,6 @@
     tx,
     rx,
     tx2,
-    rx2,
     norms,
     gram_ref,
     factor_ref,
@@ -332,7 +326,7 @@
             src_ref=tx2.at[:, device[0] * 16 + device[1]],
             dst_ref=rx2.at[me],
             send_sem=send2_sem.at[0],
-            recv_sem=recv2_sem.at[row_of(offset)],
+            recv_sem=recv2_sem.at[0],
             device_id=device,
             device_id_type=MESH,
         )
@@ -347,24 +341,6 @@
     spread_all(15, 0).wait()
     for k in range(1, 8):
         spread_group(k).start()
-
-    def arrived(m):
-        for j in range(tiles):
-            upd_v[m, :, pl.ds(j * LANES, LANES)] = rx2[m, j]
-
-    def row_arrived(dx, dy, dcore, steps):
-        part = rx2.at[pl.ds(0, len(steps))]
-        pltpu.make_async_remote_copy(
-            src_ref=part,
-            dst_ref=part,
-            send_sem=send2_sem.at[0],
-            recv_sem=recv2_sem.at[row_of((dx, dy, 0, dcore))],
-            device_id=(group, blk),
-            device_id_type=MESH,
-        ).wait_recv()
-        for dz in steps:
-            gone = shifted((lax.rem(4 - dx, 4), lax.rem(4 - dy, 4), (4 - dz) % 4, dcore))
-            arrived(gone[0] * 16 + gone[1])
 
     def fill_slots():
         spread_all(7 * 16, 1).wait()
@@ -381,20 +357,17 @@
         chosen = jnp.where(placing == me * SLOTS + lane, spread, 0.0)
         slot_ref[...] = jnp.sum(chosen, axis=0, keepdims=True)[:, :SLOTS]
 
-    for wave in range(2):
-        turn = lax.rem(core + wave, 2)
-
-        @pl.loop(0, 15)
-        def _(i):
-            row_arrived((15 - i) // 4, lax.rem(15 - i, 4), turn, (2, 1, 3, 0))
-
-        if wave == 0:
-            own2.wait()
-            arrived(me)
-            fill_slots()
-
-    row_arrived(0, 0, 0, (2, 1, 3))
-    row_arrived(0, 0, 1, (2, 1, 3, 0))
+    fill_slots()
+    own2.wait()
+    part = rx2.at[pl.ds(0, count - 1)]
+    pltpu.make_async_remote_copy(
+        src_ref=part,
+        dst_ref=part,
+        send_sem=send2_sem.at[0],
+        recv_sem=recv2_sem.at[0],
+        device_id=(group, blk),
+        device_id_type=MESH,
+    ).wait_recv()
 
     sent(count - 2 - AHEAD, send_sem.at[1]).wait_send()
     sent(1, send_sem.at[2]).wait_send()
@@ -403,6 +376,23 @@
 
 def in_hbm(array):
     return pltpu.with_memory_space_constraint(array, pltpu.HBM)
+
+
+def store_all(update, momentum_out, slots, update_hbm, momentum_hbm, slots_hbm, sems):
+    tiles = update.shape[1]
+    copies = [
+        pltpu.make_async_copy(slots, slots_hbm, sems.at[0]),
+        pltpu.make_async_copy(momentum_out, momentum_hbm, sems.at[1]),
+    ]
+    for j in range(tiles):
+        lanes = pl.ds(j * LANES, LANES)
+        copies.append(
+            pltpu.make_async_copy(update.at[:, j], update_hbm.at[:, :, lanes], sems.at[2 + j])
+        )
+    for copy in copies:
+        copy.start()
+    for copy in copies:
+        copy.wait()
 
 
 def on_device(gradient, momentum, owner_group):
@@ -413,10 +403,10 @@
     tall = (tiles, count, rows, LANES)
     square = pltpu.VMEM((full_rows, full_rows), F32)
     dma = pltpu.SemaphoreType.DMA
-    return pl.pallas_call(
+    results = pl.pallas_call(
         kernel,
         out_shape=(
-            jax.ShapeDtypeStruct(gradient.shape, BF16),
+            jax.ShapeDtypeStruct(wide, BF16),
             jax.ShapeDtypeStruct(momentum.shape, F32),
             jax.ShapeDtypeStruct((1, SLOTS), F32),
         ),
@@ -436,7 +426,6 @@
             pltpu.VMEM(wide, BF16),
             pltpu.VMEM(tall, BF16),
             pltpu.VMEM(tall, BF16),
-            pltpu.VMEM(wide, BF16),
             pltpu.VMEM((count, 1, LANES), F32),
             square,
             square,
@@ -446,7 +435,7 @@
             dma((3,)),
             dma((1,)),
             dma((1,)),
-            dma((32,)),
+            dma((1,)),
             dma((3,)),
             dma((2,)),
             dma((2,)),
@@ -457,6 +446,18 @@
             collective_id=0, has_side_effects=True, vmem_limit_bytes=44 << 20
         ),
     )(*(in_hbm(x) for x in (gradient, momentum, owner_group.reshape(1, count))))
+    return pl.pallas_call(
+        store_all,
+        out_shape=(
+            jax.ShapeDtypeStruct(gradient.shape, BF16),
+            jax.ShapeDtypeStruct(momentum.shape, F32),
+            jax.ShapeDtypeStruct((1, SLOTS), F32),
+        ),
+        in_specs=[pl.BlockSpec(memory_space=pl.ANY)] * 3,
+        out_specs=(pl.BlockSpec(memory_space=pl.ANY),) * 3,
+        scratch_shapes=[dma((2 + tiles,))],
+        compiler_params=pltpu.CompilerParams(vmem_limit_bytes=1 << 20),
+    )(*results)
 
 
 def solution(mesh):

time: 73.7 us -> 71.9 us (0.976)
  local copies, waits for them, and re-layouts: 4.1 us -> 0 us
  Pallas kernels: 68.8 us -> 71.1 us
    unnamed x3 -> x0, local copies, waits for them, and re-layouts: 4.1 us -> none
    pallas_call x1 -> x2, Pallas kernels: 68.8 us -> 71.1 us  [the longest x1 68.1 us: on_device(): pl.pallas_call(kernel, out_shape=(jax.ShapeDtypeStruct(wide, BF16), jax.S...]
where the time goes in v3:
time: 71.9 us; the launch traced here: 71.8 us
  Pallas kernels  71.1 us (99%)
    pallas_call x1, Pallas kernels, on_device(): pl.pallas_call(kernel, out_shape=(jax.ShapeDtypeStruct(wide, BF16), jax.S...  68.1 us
    pallas_call x1, Pallas kernels, on_device(): pl.pallas_call(store_all, out_shape=(jax.ShapeDtypeStruct(gradient.shape,...  3.05 us

profile of v3, /device:TPU:1, one launch (start us, length us, event | category | flops | bytes accessed | tf_op | source)
XLA Modules:
  0.0 71.8 jit_solution(4617479866488566434)
XLA Ops:
  0.6 68.1 %shard_map.58 = (bf16[128,18,4,128]{3,2,1,0:T(4,128)(2,1)S(1)}, f32[128,4,2304]{2,1,0:T(4,128)S(1)}, f32[1,2]{1,0:T(1,128)S(1)}) custom-call(bf16[128,4,2304]{2,1,0:T(4,128)(2,1)} %gradient.1, f32[128,4,2304]{2,1,0:T(4,128)} %momentum.1, s32[1,128]{1,0:T(1,128)} %bitcast.1), custom_call_target="tpu_custom_call" | custom-call | tf_op jit(solution)/shard_map/pallas_call | solution.py:406
  68.7 3.1 %shard_map.59 = (bf16[128,4,2304]{2,1,0:T(4,128)(2,1)}, f32[128,4,2304]{2,1,0:T(4,128)}, f32[1,2]{1,0:T(1,128)}) custom-call(bf16[128,18,4,128]{3,2,1,0:T(4,128)(2,1)S(1)} %get-tuple-element.6.update, f32[128,4,2304]{2,1,0:T(4,128)S(1)} %get-tuple-element.7.momentum_out, f32[1,2]{1,0:T(1,128)S(1)} %get-tuple-element.8.slots), custom_call_target="tpu_custom_call" | custom-call | tf_op jit(solution)/shard_map/pallas_call | solution.py:449

commit v4 on v3

--- a/solution.py
+++ b/solution.py
@@ -116,6 +116,7 @@
     rx,
     tx2,
     norms,
+    packed,
     gram_ref,
     factor_ref,
     turn_ref,
@@ -281,18 +282,17 @@
         )
 
     def spread_group(k):
-        part = pl.ds(group * 16, 16)
-        return pltpu.make_async_remote_copy(
-            src_ref=norms.at[part],
-            dst_ref=norms.at[part],
+        return pltpu.make_async_remote_copy(
+            src_ref=packed.at[group],
+            dst_ref=packed.at[group],
             send_sem=norm_send.at[1],
             recv_sem=norm_recv.at[1],
             device_id=(lax.rem(group + k, 8), blk),
             device_id_type=MESH,
         )
 
-    def spread_all(blocks, at):
-        part = norms.at[pl.ds(0, blocks)]
+    def spread_all(ref, blocks, at):
+        part = ref.at[pl.ds(0, blocks)]
         return pltpu.make_async_remote_copy(
             src_ref=part,
             dst_ref=part,
@@ -338,12 +338,16 @@
             back((*chip, other_core)).start()
     back((0, 0, 0, 1)).start()
 
-    spread_all(15, 0).wait()
+    spread_all(norms, 15, 0).wait()
+    sixteen = norms[pl.ds(group * 16, 16), 0, :]
+    at_row = lax.broadcasted_iota(jnp.int32, (16, LANES), 0)
+    at_lane = lax.broadcasted_iota(jnp.int32, (16, LANES), 1)
+    packed[group] = jnp.sum(jnp.where(at_row == at_lane, sixteen, 0.0), axis=0, keepdims=True)
     for k in range(1, 8):
         spread_group(k).start()
 
     def fill_slots():
-        spread_all(7 * 16, 1).wait()
+        spread_all(packed, 7, 1).wait()
 
         owners_copy.wait()
         other = jnp.broadcast_to(owners_v[...], (count, LANES))
@@ -353,7 +357,11 @@
         earlier = jnp.where((owner == other) & (lane < row), 1.0, 0.0)
         rank = jnp.sum(earlier, axis=1, keepdims=True).astype(jnp.int32)
         placing = owner * (SLOTS * 16) + rank
-        spread = norms[:, 0, :] * (1.0 / math.sqrt(full_rows * width))
+        chosen_norm = jnp.broadcast_to(
+            jnp.transpose(jnp.concatenate([packed[g][:, :16] for g in range(8)], axis=1)),
+            (count, LANES),
+        )
+        spread = chosen_norm * (1.0 / math.sqrt(full_rows * width))
         chosen = jnp.where(placing == me * SLOTS + lane, spread, 0.0)
         slot_ref[...] = jnp.sum(chosen, axis=0, keepdims=True)[:, :SLOTS]
 
@@ -427,6 +435,7 @@
             pltpu.VMEM(tall, BF16),
             pltpu.VMEM(tall, BF16),
             pltpu.VMEM((count, 1, LANES), F32),
+            pltpu.VMEM((8, 1, LANES), F32),
             square,
             square,
             square,

time: 71.9 us -> 71.3 us (level)
  no operation moved by 1% of the time
where the time goes in v4:
time: 71.3 us; the launch traced here: 71.2 us
  Pallas kernels  70.6 us (99%)
    pallas_call x1, Pallas kernels, on_device(): pl.pallas_call(kernel, out_shape=(jax.ShapeDtypeStruct(wide, BF16), jax.S...  67.5 us
    pallas_call x1, Pallas kernels, on_device(): pl.pallas_call(store_all, out_shape=(jax.ShapeDtypeStruct(gradient.shape,...  3.05 us

profile of v4, /device:TPU:1, one launch (start us, length us, event | category | flops | bytes accessed | tf_op | source)
XLA Modules:
  0.0 71.2 jit_solution(15688635693243779581)
XLA Ops:
  0.6 67.5 %shard_map.58 = (bf16[128,18,4,128]{3,2,1,0:T(4,128)(2,1)S(1)}, f32[128,4,2304]{2,1,0:T(4,128)S(1)}, f32[1,2]{1,0:T(1,128)S(1)}) custom-call(bf16[128,4,2304]{2,1,0:T(4,128)(2,1)} %gradient.1, f32[128,4,2304]{2,1,0:T(4,128)} %momentum.1, s32[1,128]{1,0:T(1,128)} %bitcast.1), custom_call_target="tpu_custom_call" | custom-call | tf_op jit(solution)/shard_map/pallas_call | solution.py:414
  68.2 3.1 %shard_map.59 = (bf16[128,4,2304]{2,1,0:T(4,128)(2,1)}, f32[128,4,2304]{2,1,0:T(4,128)}, f32[1,2]{1,0:T(1,128)}) custom-call(bf16[128,18,4,128]{3,2,1,0:T(4,128)(2,1)S(1)} %get-tuple-element.6.update, f32[128,4,2304]{2,1,0:T(4,128)S(1)} %get-tuple-element.7.momentum_out, f32[1,2]{1,0:T(1,128)S(1)} %get-tuple-element.8.slots), custom_call_target="tpu_custom_call" | custom-call | tf_op jit(solution)/shard_map/pallas_call | solution.py:458
